TPU v7x, 32 devices: a whole 2x2x4 slice. The times are simulated.
32 devices in a mesh: ctx: 4 (over z), exp: 8 (over y, x, core).
Axes of the slice: x: 2, y: 2, z: 4, core: 2. Of those that a mesh axis runs over, the one named last changes fastest.
Arguments:
- queries: bfloat16 [256, 3072], P('ctx', 'exp'), may hold values from -8 to 8
- keys_values: bfloat16 [2, 256, 512], P(None, 'ctx', 'exp'), may hold values from -8 to 8
- residual: bfloat16 [256, 6144], P(('ctx', 'exp')), may hold values from -12 to 12
- out_weight: bfloat16 [3072, 6144], P('exp', 'ctx'), may hold values from -0.109375 to 0.109375
- norm_gain: float32 [6144], replicated, may hold values from 0.5 to 2
- routes: int32 [256, 4], P(('ctx', 'exp')), may hold values from 0 to 7, as said below
- route_weight: float32 [256, 4], P(('ctx', 'exp')), may hold values from 0.1 to 1
- gate_weight: bfloat16 [8, 6144, 5376], P('exp', None, 'ctx'), may hold values from -0.078125 to 0.078125
- up_weight: bfloat16 [8, 6144, 5376], P('exp', None, 'ctx'), may hold values from -0.078125 to 0.078125
- down_weight: bfloat16 [8, 5376, 6144], P('exp', 'ctx'), may hold values from -0.078125 to 0.078125
Outputs:
- layer_out: bfloat16 [256, 6144], P(('ctx', 'exp'))
Inputs may be any that keep to these rules, and one draw needn't show every extreme that they name: `routes`: each row names 4 different experts. Within each aligned block of 8 rows (the rows of one device) no expert is named by more than 8 rows, and one expert is named by exactly 8 rows in every block.
All inputs are finite; a program needn't handle non-finite values.
Results may differ from a plain program's by a relative error of at most 0.025.
Values may be sent and summed in bfloat16 or wider, within the bound.
No kernel may reach another device: no remote copies, remote signals or barrier semaphores. Data moves between devices by JAX's collectives and lax.ppermute only.
A program may use at most 128 MiB of HBM per device.

v0:
```python
import math

import jax
import jax.numpy as jnp
from jax import lax
from jax.sharding import PartitionSpec as P

HD = 128


def from_partner(value, axis, bit):
    return lax.ppermute(value, axis, [(i, i ^ 1 << bit) for i in range(lax.axis_size(axis))])


def expert_partial(token_block, gate_weight, up_weight, down_weight):
    gate_part = jnp.einsum(
        "ind,df->inf", token_block, gate_weight[0], preferred_element_type=jnp.float32
    )
    up_part = jnp.einsum(
        "ind,df->inf", token_block, up_weight[0], preferred_element_type=jnp.float32
    )
    activated = (jax.nn.silu(gate_part) * up_part).astype(jnp.bfloat16)
    return jnp.einsum("inf,fd->ind", activated, down_weight[0], preferred_element_type=jnp.float32)


def on_device(
    queries,
    keys_values,
    residual,
    out_weight,
    norm_gain,
    routes,
    route_weight,
    gate_weight,
    up_weight,
    down_weight,
):
    context_devices = lax.axis_size("ctx")
    expert_devices = lax.axis_size("exp")
    block_rows = queries.shape[0]
    local_heads = queries.shape[1] // HD
    token_rows = residual.shape[0]
    features = residual.shape[1]
    partner = from_partner(keys_values, "exp", 0)
    is_lower = lax.axis_index("exp") % 2 == 0
    joined = jnp.where(
        is_lower,
        jnp.concatenate([keys_values, partner], axis=2),
        jnp.concatenate([partner, keys_values], axis=2),
    )
    query_heads = queries.reshape(block_rows, local_heads, HD)
    first_position = lax.axis_index("ctx") * block_rows
    query_position = first_position + jnp.arange(block_rows, dtype=jnp.int32)
    last_position = first_position + block_rows - 1
    initial = (
        jnp.full((local_heads, block_rows), -jnp.inf, jnp.float32),
        jnp.zeros((local_heads, block_rows), jnp.float32),
        jnp.zeros((local_heads, block_rows, HD), jnp.float32),
    )
    portion = lax.all_gather(joined, "ctx", axis=1, tiled=True)

    def update(current):
        running_max, denominator, weighted_sum = current
        scores = jnp.einsum(
            "qhd,kd->hqk", query_heads, portion[0], preferred_element_type=jnp.float32
        ) / math.sqrt(HD)
        key_position = jnp.arange(portion.shape[1], dtype=jnp.int32)
        allowed = key_position[None, None, :] <= query_position[None, :, None]
        masked = jnp.where(allowed, scores, -jnp.inf)
        new_max = jnp.max(masked, axis=2)
        safe_max = jnp.where(new_max == -jnp.inf, 0.0, new_max)
        weights_now = jnp.where(allowed, jnp.exp(masked - safe_max[:, :, None]), 0.0)
        rescale = jnp.exp(running_max - safe_max)
        denominator = rescale * denominator + jnp.sum(weights_now, axis=2)
        weighted_sum = rescale[:, :, None] * weighted_sum + jnp.einsum(
            "hqk,kd->hqd",
            weights_now,
            portion[1].astype(jnp.float32),
            precision=lax.Precision.HIGHEST,
        )
        return (new_max, denominator, weighted_sum)

    running_max, denominator, weighted_sum = lax.cond(
        jnp.int32(0) > last_position, lambda unchanged: unchanged, update, initial
    )
    attended = (
        (weighted_sum / denominator[:, :, None])
        .transpose(1, 0, 2)
        .reshape(block_rows, local_heads * HD)
        .astype(jnp.bfloat16)
    )
    partial_value = jnp.dot(
        attended,
        lax.all_gather(out_weight, "ctx", axis=1, tiled=True),
        preferred_element_type=jnp.float32,
    )
    projected = lax.psum_scatter(
        partial_value.astype(jnp.bfloat16), "exp", scatter_dimension=0, tiled=True
    ).astype(jnp.float32)
    hidden_state = residual.astype(jnp.float32) + projected
    row_mean = jnp.mean(hidden_state, axis=1, keepdims=True)
    centered = hidden_state - row_mean
    variance = jnp.mean(centered * centered, axis=1, keepdims=True)
    normed = (centered * lax.rsqrt(variance + 1e-05) * norm_gain).astype(jnp.bfloat16)
    fanout = routes.shape[1]
    capacity = 2 * token_rows * fanout // expert_devices
    flat_routes = routes.reshape(-1)
    selector = (
        flat_routes[:, None] == jnp.arange(expert_devices, dtype=jnp.int32)[None, :]
    ).astype(jnp.int32)
    earlier = jnp.cumsum(selector, axis=0) - selector
    slot_index = jnp.sum(earlier * selector, axis=1)
    target = flat_routes * capacity + slot_index
    source_rows = jnp.repeat(normed, fanout, axis=0)
    packed = (
        jnp.zeros((expert_devices * capacity, features), jnp.bfloat16).at[target].set(source_rows)
    )
    spread = jnp.broadcast_to(
        packed.reshape(1, expert_devices, capacity, features),
        (context_devices, expert_devices, capacity, features),
    )
    spread = spread.reshape(context_devices * expert_devices, capacity, features)
    partial_out = expert_partial(
        lax.all_to_all(spread, ("ctx", "exp"), split_axis=0, concat_axis=0, tiled=True),
        gate_weight,
        up_weight,
        down_weight,
    ).astype(jnp.bfloat16)
    returned = lax.all_to_all(partial_out, ("ctx", "exp"), split_axis=0, concat_axis=0, tiled=True)
    combined = jnp.sum(
        returned.reshape(context_devices, expert_devices * capacity, features).astype(jnp.float32),
        axis=0,
    )
    expert_out = combined[target]
    weighted = (expert_out * route_weight.reshape(-1)[:, None]).reshape(
        token_rows, fanout, features
    )
    return (hidden_state + jnp.sum(weighted, axis=1)).astype(jnp.bfloat16)


def solution(mesh):
    in_specs = (
        P("ctx", "exp"),
        P(None, "ctx", "exp"),
        P(("ctx", "exp"), None),
        P("exp", "ctx"),
        P(),
        P(("ctx", "exp"), None),
        P(("ctx", "exp"), None),
        P("exp", None, "ctx"),
        P("exp", None, "ctx"),
        P("exp", "ctx", None),
    )
    out_specs = P(("ctx", "exp"), None)
    return jax.shard_map(
        on_device, mesh=mesh, in_specs=in_specs, out_specs=out_specs, check_vma=False
    )
```

profile of v0, /device:TPU:0, one launch (start us, length us, event | category | flops | bytes accessed | tf_op | source)
XLA Modules:
  0.0 336.0 jit_solution(835207451480851856)
XLA Ops:
  6.5 0.7 all-gather.2.cloned.1.call-update
  7.3 0.5 collective-permute-start
  7.8 1.1 collective-permute-done
  8.9 0.9 maximum_select_fusion
  9.8 15.1 %all_gather.6 = bf16[2,256,128]{2,1,0:T(8,128)(2,1)S(1)} all-gather(bf16[2,64,128]{2,1,0:T(8,128)(2,1)S(1)} %maximum_select_fusion), channel_id=1, replica_groups=mesh['ctx'=4,'exp'=8] {'ctx'}, dimensions={1}, use_global_device_ids=true | all-gather | bytes 163840 | tf_op jit(solution)/shard_map/all_gather | solution.py:60
  24.9 1.7 conditional.1
  25.0 1.1 fusion.46
  26.1 0.2 fusion.2
  26.3 0.3 convolution_add_fusion
  26.6 74.8 %all-gather.2.cloned.1.call-done = bf16[384,6144]{1,0:T(8,128)(2,1)} async-done(((bf16[384,1536]{1,0:T(8,128)(2,1)}), bf16[384,6144]{1,0:T(8,128)(2,1)}) %all-gather.2.cloned.1.call-update) | async-done | bytes 4718608 | tf_op jit(solution)/shard_map/all_gather | solution.py:94
  101.4 4.3 %convolution_convert_fusion = bf16[64,6144]{1,0:T(8,128)(2,1)} fusion(bf16[384,6144]{1,0:T(8,128)(2,1)} %all-gather.2.cloned.1.call-done, f32[3,64,128]{2,1,0:T(8,128)S(1)} %get-tuple-element.22, f32[3,64]{1,0:T(4,128)S(1)} %get-tuple-element.23), kind=kOutput, calls=%fused_computation.30 | convolution fusion | flops 302432256 | bytes 5604096 | tf_op jit(solution)/shard_map/dot_general | solution.py:92
  106.0 0.1 copy.18
  106.1 0.2 select_reduce_fusion
  106.3 32.9 %reduce-scatter.2.cloned.1.call-done = bf16[8,6144]{1,0:T(8,128)(2,1)} async-done(((bf16[64,6144]{1,0:T(8,128)(2,1)}), bf16[8,6144]{1,0:T(8,128)(2,1)}) %reduce-scatter.2.cloned.1.call-update) | async-done | bytes 98320 | tf_op jit(solution)/shard_map/reduce_scatter | solution.py:97
  139.3 1.1 fusion.39
  140.3 1.1 multiply_reduce_fusion.1
  141.5 1.0 multiply_convert_fusion
  142.5 0.1 broadcast_in_dim.55
  142.6 0.1 reshape.114
  142.7 1.4 scatter_custom_fusion
  144.1 0.4 broadcast_in_dim.57
  144.4 75.6 %all_to_all.10 = bf16[32,8,6144]{2,1,0:T(8,128)(2,1)S(1)} all-to-all(bf16[32,8,6144]{2,1,0:T(8,128)(2,1)S(1)} %bitcast.67), channel_id=1, replica_groups=mesh['ctx'=4,'exp'=8] {'ctx','exp'}, dimensions={0} | all-to-all | bytes 6291456 | tf_op jit(solution)/shard_map/all_to_all | solution.py:124
  220.0 9.7 %fusion.18 = f32[32,8,1344]{2,1,0:T(8,128)} fusion(bf16[32,8,6144]{2,1,0:T(8,128)(2,1)S(1)} %all_to_all.10, bf16[1,6144,1344]{1,2,0:T(8,128)(2,1)} %param.19), kind=kOutput, calls=%fused_computation.27 | convolution fusion | flops 4227858432 | bytes 21037056 | tf_op jit(solution)/shard_map/ind,df->inf/dot_general | solution.py:16
  229.7 17.7 %fusion.20 = bf16[32,8,6144]{2,1,0:T(8,128)(2,1)} fusion(bf16[1,1344,6144]{2,1,0:T(8,128)(2,1)} %param.21, bf16[32,8,6144]{2,1,0:T(8,128)(2,1)S(1)} %all_to_all.10, bf16[1,6144,1344]{1,2,0:T(8,128)(2,1)} %param.20, f32[32,8,1344]{2,1,0:T(8,128)} %fusion.18), kind=kOutput, calls=%fused_computation.29 | convolution fusion | flops 8459354112 | bytes 40697856 | tf_op jit(solution)/shard_map/inf,fd->ind/dot_general | solution.py:23
  247.5 3.7 %all-to-all-start.1 = ((bf16[32,8,6144]{2,1,0:T(8,128)(2,1)}), bf16[32,8,6144]{2,1,0:T(8,128)(2,1)S(1)}, u32[]{:S(2)}, u32[]{:S(2)}) async-start(bf16[32,8,6144]{2,1,0:T(8,128)(2,1)} %fusion.20), calls=%async_computation.2 | async-start | bytes 6291456 | tf_op jit(solution)/shard_map/all_to_all | solution.py:129
  251.2 71.4 %all-to-all-done.1 = bf16[32,8,6144]{2,1,0:T(8,128)(2,1)S(1)} async-done(((bf16[32,8,6144]{2,1,0:T(8,128)(2,1)}), bf16[32,8,6144]{2,1,0:T(8,128)(2,1)S(1)}, u32[]{:S(2)}, u32[]{:S(2)}) %all-to-all-start.1) | async-done | bytes 3145760 | tf_op jit(solution)/shard_map/all_to_all | solution.py:129
  322.6 1.7 copy-done
  324.3 2.5 convert_reduce_fusion
  326.8 0.8 gather_fusion
  327.6 0.2 gather.6
  327.9 0.6 multiply_reduce_fusion
  328.4 0.7 add_convert_fusion
  (30 shorter events, 0.7 us)
Async XLA Ops:
  6.5 94.8 %all-gather.2.cloned.1.call-start = ((), (), s32[]{:S(2)}) async-start(), calls=%async_computation.3 | async-start | bytes 5898240 | tf_op jit(solution)/shard_map/all_gather | solution.py:94
  7.3 132.0 %reduce-scatter.2.cloned.1.call-start = ((), (), s32[]{:S(2)}) async-start(), calls=%async_computation.4 | async-start | bytes 884736 | tf_op jit(solution)/shard_map/reduce_scatter | solution.py:97
  7.3 1.6 collective-permute-start
  101.4 4.3 %copy-start.4 = (s32[8,4]{0,1:T(4,128)S(1)}, s32[8,4]{0,1:T(4,128)}, u32[]{:S(2)}) copy-start(s32[8,4]{0,1:T(4,128)} %param.17) | copy-start | bytes 388
  101.4 37.9 %copy-start.1 = (bf16[8,6144]{1,0:T(8,128)(2,1)S(1)}, bf16[8,6144]{1,0:T(8,128)(2,1)}, u32[]{:S(2)}) copy-start(bf16[8,6144]{1,0:T(8,128)(2,1)} %param.14) | copy-start | bytes 294916
  101.4 40.1 %copy-start.3 = (f32[6144]{0:T(1024)S(1)}, f32[6144]{0:T(1024)}, u32[]{:S(2)}) copy-start(f32[6144]{0:T(1024)} %param.16) | copy-start | bytes 73732
  247.5 3.7 %copy-start.5 = (f32[8,4]{0,1:T(4,128)S(1)}, f32[8,4]{0,1:T(4,128)}, u32[]{:S(2)}) copy-start(f32[8,4]{0,1:T(4,128)} %param.18) | copy-start | bytes 388
  247.5 75.1 %all-to-all-start.1 = ((bf16[32,8,6144]{2,1,0:T(8,128)(2,1)}), bf16[32,8,6144]{2,1,0:T(8,128)(2,1)S(1)}, u32[]{:S(2)}, u32[]{:S(2)}) async-start(bf16[32,8,6144]{2,1,0:T(8,128)(2,1)} %fusion.20), calls=%async_computation.2 | async-start | bytes 6291456 | tf_op jit(solution)/shard_map/all_to_all | solution.py:129
  322.6 1.7 copy-start
  326.8 1.6 copy-start.2
Sparse Core Ops, SparseCore 0:
  8.9 92.4 all-gather.1
  105.8 33.4 reduce-scatter.1
where the time goes:
time: 336 us
  waiting for transfers between devices  181 us (54%)
  blocking collectives  90.6 us (27%)
  matrix products  33.1 us (10%)
  between operations  13.5 us (4%)
  other arithmetic  8.49 us (3%)
  local copies, waits for them, and re-layouts  5.07 us (2%)
  starting transfers between devices  4.23 us (1%)
    all_to_all x1, blocking collectives, on_device(): lax.all_to_all(spread, ('ctx', 'exp'), split_axis=0, concat_axis=0, tiled...  75.6 us
    all_gather x1, waiting for transfers between devices, on_device(): lax.all_gather(out_weight, 'ctx', axis=1, tiled=True)  74.8 us
    all_to_all x1, waiting for transfers between devices, on_device(): lax.all_to_all(partial_out, ('ctx', 'exp'), split_axis=0, concat_axis=0,...  71.4 us
    reduce_scatter x1, waiting for transfers between devices, on_device(): lax.psum_scatter(partial_value.astype(jnp.bfloat16), 'exp', scatter_dimen...  32.9 us
    dot_general x1, matrix products, expert_partial(): jnp.einsum('inf,fd->ind', activated, down_weight[0], preferred_element_ty...  17.7 us
    all_gather x1, blocking collectives, on_device(): portion = lax.all_gather(joined, 'ctx', axis=1, tiled=True)  15.1 us
    dot_general x1, matrix products, expert_partial(): jnp.einsum('ind,df->inf', token_block, gate_weight[0], preferred_element_...  9.72 us
  transfers between devices with their start and end apart: 4, of which 4 were waited for; matrix products, arithmetic and copies ran while one was open for 1% of the time, Pallas kernels for 0%

commit v1 on v0

v1 whole, which is shorter than its diff:
```python
import math

import jax
import jax.numpy as jnp
from jax import lax
from jax.sharding import PartitionSpec as P

HD = 128


def from_partner(value, axis, bit):
    return lax.ppermute(value, axis, [(i, i ^ 1 << bit) for i in range(lax.axis_size(axis))])


def on_device(
    queries,
    keys_values,
    residual,
    out_weight,
    norm_gain,
    routes,
    route_weight,
    gate_weight,
    up_weight,
    down_weight,
):
    C = lax.axis_size("ctx")
    E = lax.axis_size("exp")
    block_rows = queries.shape[0]
    heads = queries.shape[1] // HD
    seq = block_rows * C
    token_rows, features = residual.shape
    partner = from_partner(keys_values, "exp", 0)
    is_lower = lax.axis_index("exp") % 2 == 0
    joined = jnp.where(
        is_lower,
        jnp.concatenate([keys_values, partner], axis=2),
        jnp.concatenate([partner, keys_values], axis=2),
    )
    kv = lax.all_gather(joined, "ctx", axis=1, tiled=True)
    q = lax.all_gather(queries, "ctx", axis=0, tiled=True).reshape(seq, heads, HD)
    experts = jnp.arange(E, dtype=jnp.int32)
    own_weights = jnp.sum(
        jnp.where(routes[:, :, None] == experts, route_weight[:, :, None], 0.0), axis=1
    )
    all_weights = lax.all_gather(own_weights, ("ctx", "exp"), axis=0, tiled=True)
    scores = jnp.einsum("qhd,kd->hqk", q, kv[0], preferred_element_type=jnp.float32) / math.sqrt(HD)
    position = jnp.arange(seq, dtype=jnp.int32)
    scores = jnp.where(position[None, None, :] <= position[None, :, None], scores, -jnp.inf)
    top = jnp.max(scores, axis=2, keepdims=True)
    weights = jnp.exp(scores - top)
    total = jnp.sum(weights, axis=2, keepdims=True)
    summed = jnp.einsum(
        "hqk,kd->hqd",
        weights,
        kv[1].astype(jnp.float32),
        precision=lax.Precision.HIGHEST,
        preferred_element_type=jnp.float32,
    )
    attended = (summed / total).transpose(1, 0, 2).reshape(seq, heads * HD).astype(jnp.bfloat16)
    partial_value = jnp.dot(attended, out_weight, preferred_element_type=jnp.float32)
    blocks = partial_value.astype(jnp.bfloat16).reshape(C, E, token_rows, -1).transpose(1, 0, 2, 3)
    blocks = blocks.reshape(seq, -1)
    mine = lax.psum_scatter(blocks, "exp", scatter_dimension=0, tiled=True)
    mine = mine.reshape(C, token_rows, -1)
    projected = lax.all_to_all(mine, "ctx", split_axis=0, concat_axis=2, tiled=True)
    hidden_state = residual.astype(jnp.float32) + projected.reshape(token_rows, features).astype(
        jnp.float32
    )
    row_mean = jnp.mean(hidden_state, axis=1, keepdims=True)
    centered = hidden_state - row_mean
    variance = jnp.mean(centered * centered, axis=1, keepdims=True)
    normed = (centered * lax.rsqrt(variance + 1e-05) * norm_gain).astype(jnp.bfloat16)
    rows = lax.all_gather(normed, ("ctx", "exp"), axis=0, tiled=True)
    gate_part = jnp.dot(rows, gate_weight[0], preferred_element_type=jnp.float32)
    up_part = jnp.dot(rows, up_weight[0], preferred_element_type=jnp.float32)
    activated = (jax.nn.silu(gate_part) * up_part).astype(jnp.bfloat16)
    piece = jnp.dot(activated, down_weight[0], preferred_element_type=jnp.float32)
    mine_only = (lax.axis_index("exp") == experts).astype(jnp.float32)
    scale = jnp.sum(all_weights * mine_only, axis=1, keepdims=True)
    weighted = (piece * scale).astype(jnp.bfloat16)
    combined = lax.psum_scatter(weighted, ("ctx", "exp"), scatter_dimension=0, tiled=True)
    return (hidden_state + combined.astype(jnp.float32)).astype(jnp.bfloat16)


def solution(mesh):
    in_specs = (
        P("ctx", "exp"),
        P(None, "ctx", "exp"),
        P(("ctx", "exp"), None),
        P("exp", "ctx"),
        P(),
        P(("ctx", "exp"), None),
        P(("ctx", "exp"), None),
        P("exp", None, "ctx"),
        P("exp", None, "ctx"),
        P("exp", "ctx", None),
    )
    out_specs = P(("ctx", "exp"), None)
    return jax.shard_map(
        on_device, mesh=mesh, in_specs=in_specs, out_specs=out_specs, check_vma=False
    )
```

time: 336 us -> 294 us (0.88)
  waiting for transfers between devices: 181 us -> 155 us
  blocking collectives: 90.6 us -> 77.8 us
  matrix products: 33.1 us -> 41.7 us
  other arithmetic: 8.49 us -> 3.99 us
  local copies, waits for them, and re-layouts: 5.07 us -> 1.18 us
  starting transfers between devices: 4.23 us -> 0.54 us
    reduce_scatter x1 -> x2, waiting for transfers between devices: 32.9 us -> 137 us  [the longest x1 100 us: on_device(): lax.psum_scatter(weighted, ('ctx', 'exp'), scatter_dimension=0, tiled=True)]
    all_to_all x1 -> x0, waiting for transfers between devices: 71.4 us -> none  [on_device(): lax.all_to_all(partial_out, ('ctx', 'exp'), split_axis=0, concat_axis=0,...]
    all_to_all x1, blocking collectives: 75.6 us -> 10.4 us  [on_device(): lax.all_to_all(mine, 'ctx', split_axis=0, concat_axis=2, tiled=True)]
    all_gather x1, waiting for transfers between devices: 74.8 us -> 18 us  [on_device(): rows = lax.all_gather(normed, ('ctx', 'exp'), axis=0, tiled=True)]
    all_gather x1 -> x3, blocking collectives: 15.1 us -> 67.4 us  [the longest x1 38.7 us: on_device(): lax.all_gather(own_weights, ('ctx', 'exp'), axis=0, tiled=True)]
    dot_general x5, matrix products: 33.1 us -> 41.7 us  [the longest x1 31.2 us: on_device(): jnp.dot(activated, down_weight[0], preferred_element_type=jnp.float32)]
    all_to_all x1 -> x0, starting transfers between devices: 3.67 us -> none  [on_device(): lax.all_to_all(partial_out, ('ctx', 'exp'), split_axis=0, concat_axis=0,...]
  transfers between devices with their start and end apart: 4 -> 4, of which waited for: 4 -> 3; matrix products, arithmetic and copies ran while one was open for 1% -> 0% of each run, Pallas kernels for 0% -> 0%
where the time goes in v1:
time: 294 us; the launch traced here: 293 us
  waiting for transfers between devices  155 us (53%)
  blocking collectives  77.8 us (26%)
  matrix products  41.7 us (14%)
  between operations  13.2 us (4%)
  other arithmetic  3.99 us (1%)
    reduce_scatter x1, waiting for transfers between devices, on_device(): lax.psum_scatter(weighted, ('ctx', 'exp'), scatter_dimension=0, tiled=True)  100 us
    all_gather x1, blocking collectives, on_device(): lax.all_gather(own_weights, ('ctx', 'exp'), axis=0, tiled=True)  38.7 us
    reduce_scatter x1, waiting for transfers between devices, on_device(): mine = lax.psum_scatter(blocks, 'exp', scatter_dimension=0, tiled=True)  36.4 us
    dot_general x1, matrix products, on_device(): jnp.dot(activated, down_weight[0], preferred_element_type=jnp.float32)  31.2 us
    all_gather x1, waiting for transfers between devices, on_device(): rows = lax.all_gather(normed, ('ctx', 'exp'), axis=0, tiled=True)  18 us
    all_gather x1, blocking collectives, on_device(): lax.all_gather(queries, 'ctx', axis=0, tiled=True).reshape(seq, heads, HD)  15.3 us
    all_gather x1, blocking collectives, on_device(): kv = lax.all_gather(joined, 'ctx', axis=1, tiled=True)  13.4 us
    all_to_all x1, blocking collectives, on_device(): lax.all_to_all(mine, 'ctx', split_axis=0, concat_axis=2, tiled=True)  10.4 us
  transfers between devices with their start and end apart: 4, of which 3 were waited for; matrix products, arithmetic and copies ran while one was open for 0% of the time, Pallas kernels for 0%

profile of v1, /device:TPU:0, one launch (start us, length us, event | category | flops | bytes accessed | tf_op | source)
XLA Modules:
  0.0 293.4 jit_solution(5485483243851116985)
XLA Ops:
  6.5 0.5 collective-permute-start
  7.0 15.3 %all_gather.13 = bf16[256,384]{1,0:T(8,128)(2,1)S(1)} all-gather(bf16[64,384]{1,0:T(8,128)(2,1)} %param.10), channel_id=1, replica_groups=mesh['ctx'=4,'exp'=8] {'ctx'}, dimensions={0}, use_global_device_ids=true | all-gather | bytes 245760 | tf_op jit(solution)/shard_map/all_gather | solution.py:41
  22.3 0.1 copy.41
  22.4 0.9 maximum_select_fusion
  23.4 13.4 %all_gather.12 = bf16[2,256,128]{2,1,0:T(8,128)(2,1)S(1)} all-gather(bf16[2,64,128]{2,1,0:T(8,128)(2,1)S(1)} %maximum_select_fusion), channel_id=1, replica_groups=mesh['ctx'=4,'exp'=8] {'ctx'}, dimensions={1}, use_global_device_ids=true | all-gather | bytes 163840 | tf_op jit(solution)/shard_map/all_gather | solution.py:40
  36.8 0.3 fusion.25
  37.1 0.1 fusion.22
  37.2 0.0 copy-start.1
  37.2 0.5 fusion.21
  37.8 0.0 copy-start.3
  37.8 0.0 copy-start.4
  37.8 0.6 convolution_convert_fusion
  38.4 0.9 copy.45
  39.3 0.0 reduce-scatter.3.cloned.1.call-update
  39.4 0.0 all-gather.2.cloned.1.call-start
  39.4 36.4 %reduce-scatter.3.cloned.1.call-done = bf16[32,1536]{1,0:T(8,128)(2,1)} async-done(((bf16[256,1536]{1,0:T(8,128)(2,1)}), bf16[32,1536]{1,0:T(8,128)(2,1)}) %reduce-scatter.3.cloned.1.call-update) | async-done | bytes 98320 | tf_op jit(solution)/shard_map/reduce_scatter | solution.py:64
  75.9 10.4 %all_to_all.4 = bf16[4,8,1536]{2,1,0:T(8,128)(2,1)S(1)} all-to-all(bf16[4,8,1536]{2,1,0:T(8,128)(2,1)} %bitcast.74), channel_id=1, replica_groups=mesh['ctx'=4,'exp'=8] {'ctx'}, dimensions={0} | all-to-all | bytes 196608 | tf_op jit(solution)/shard_map/all_to_all | solution.py:66
  86.3 0.2 fusion.24
  86.5 0.2 multiply_reduce_fusion
  86.8 0.7 multiply_convert_fusion
  87.5 0.0 all-gather.2.cloned.1.call-update
  87.5 0.0 reduce-scatter.5.cloned.1.call-start
  87.6 0.1 select_reduce_fusion
  87.7 38.7 %all_gather.15 = f32[256,8]{1,0:T(8,128)S(1)} all-gather(f32[8,8]{1,0:T(8,128)S(1)} %select_reduce_fusion), channel_id=1, replica_groups=mesh['ctx'=4,'exp'=8] {'ctx','exp'}, dimensions={0}, use_global_device_ids=true | all-gather | bytes 8448 | tf_op jit(solution)/shard_map/all_gather | solution.py:46
  126.4 0.1 copy.46
  126.4 0.1 multiply_reduce_fusion.1
  126.5 18.0 %all-gather.2.cloned.1.call-done = bf16[256,6144]{1,0:T(8,128)(2,1)} async-done(((bf16[8,6144]{1,0:T(8,128)(2,1)}), bf16[256,6144]{1,0:T(8,128)(2,1)}) %all-gather.2.cloned.1.call-update) | async-done | bytes 3145744 | tf_op jit(solution)/shard_map/all_gather | solution.py:74
  144.5 9.1 %fusion.4 = f32[256,1344]{0,1:T(8,128)S(1)} fusion(bf16[256,6144]{1,0:T(8,128)(2,1)} %all-gather.2.cloned.1.call-done, bf16[1,6144,1344]{1,2,0:T(8,128)(2,1)} %param.17), kind=kOutput, calls=%fused_computation.4 | convolution fusion | flops 4227858432 | bytes 21037056 | tf_op jit(solution)/shard_map/dot_general | solution.py:75
  153.7 31.2 %fusion.9 = bf16[256,6144]{1,0:T(8,128)(2,1)} fusion(bf16[1,1344,6144]{2,1,0:T(8,128)(2,1)} %param.19, f32[256]{0:T(256)S(1)} %multiply_reduce_fusion.1, bf16[256,6144]{1,0:T(8,128)(2,1)} %all-gather.2.cloned.1.call-done, bf16[1,6144,1344]{1,2,0:T(8,128)(2,1)} %param.18, f32[256,1344]{0,1:T(8,128)S(1)} %fusion.4), kind=kOutput, calls=%fused_computation.7 | convolution fusion | flops 8460926976 | bytes 40698880 | tf_op jit(solution)/shard_map/dot_general | solution.py:78
  184.8 0.0 reduce-scatter.5.cloned.1.call-update
  184.9 100.5 %reduce-scatter.5.cloned.1.call-done = bf16[8,6144]{1,0:T(8,128)(2,1)} async-done(((bf16[256,6144]{1,0:T(8,128)(2,1)}), bf16[8,6144]{1,0:T(8,128)(2,1)}) %reduce-scatter.5.cloned.1.call-update) | async-done | bytes 98320 | tf_op jit(solution)/shard_map/reduce_scatter | solution.py:82
  285.3 1.6 add_convert_fusion
  (14 shorter events, 0.1 us)
Async XLA Ops:
  6.5 31.3 %copy-start = (bf16[384,1536]{1,0:T(8,128)(2,1)S(1)}, bf16[384,1536]{1,0:T(8,128)(2,1)}, u32[]{:S(2)}) copy-start(bf16[384,1536]{1,0:T(8,128)(2,1)} %param.13) | copy-start | bytes 3538948
  6.5 69.3 %reduce-scatter.3.cloned.1.call-start = ((), (), s32[]{:S(2)}) async-start(), calls=%async_computation.3 | async-start | bytes 884736 | tf_op jit(solution)/shard_map/reduce_scatter | solution.py:64
  6.5 15.9 %collective-permute-start = (bf16[2,64,64]{2,1,0:T(8,128)(2,1)}, bf16[2,64,64]{2,1,0:T(8,128)(2,1)S(1)}, u32[]{:S(2)}, u32[]{:S(2)}) collective-permute-start(bf16[2,64,64]{2,1,0:T(8,128)(2,1)} %param.11), channel_id=1, source_target_pairs={{0,1},{1,0},{2,3},{3,2},{4,5},{5,4},{6,7},{7,6},{8,9},{9,8},{10,11... | collective-permute-start | bytes 49160 | tf_op jit(solution)/shard_map/ppermute | solution.py:12
  37.2 49.1 %copy-start.1 = (bf16[8,6144]{1,0:T(8,128)(2,1)S(1)}, bf16[8,6144]{1,0:T(8,128)(2,1)}, u32[]{:S(2)}) copy-start(bf16[8,6144]{1,0:T(8,128)(2,1)} %param.12) | copy-start | bytes 294916
  37.8 49.0 %copy-start.2 = (f32[6144]{0:T(1024)S(1)}, f32[6144]{0:T(1024)}, u32[]{:S(2)}) copy-start(f32[6144]{0:T(1024)} %param.14) | copy-start | bytes 73732
  37.8 49.8 %copy-start.3 = (f32[8,4]{0,1:T(4,128)S(1)}, f32[8,4]{0,1:T(4,128)}, u32[]{:S(2)}) copy-start(f32[8,4]{0,1:T(4,128)} %param.16) | copy-start | bytes 388
  37.8 49.8 %copy-start.4 = (s32[8,4]{0,1:T(4,128)S(1)}, s32[8,4]{0,1:T(4,128)}, u32[]{:S(2)}) copy-start(s32[8,4]{0,1:T(4,128)} %param.15) | copy-start | bytes 388
  39.4 105.2 %all-gather.2.cloned.1.call-start = ((), (), s32[]{:S(2)}) async-start(), calls=%async_computation.4 | async-start | bytes 3244032 | tf_op jit(solution)/shard_map/all_gather | solution.py:74
  87.5 197.8 %reduce-scatter.5.cloned.1.call-start = ((), (), s32[]{:S(2)}) async-start(), calls=%async_computation.5 | async-start | bytes 3244032 | tf_op jit(solution)/shard_map/reduce_scatter | solution.py:82
Sparse Core Ops, SparseCore 0:
  39.5 36.3 reduce-scatter.2
  87.6 56.8 all-gather.1
  185.0 100.3 reduce-scatter.4

commit v2 on v1

v2 whole, which is shorter than its diff:
```python
import functools
import math

import jax
import jax.numpy as jnp
from jax import lax
from jax.experimental import pallas as pl
from jax.experimental.pallas import tpu as pltpu
from jax.sharding import PartitionSpec as P

HD = 128
EXTRA = 128
SPLIT = 3
VMEM_LIMIT = 56 * 1024 * 1024
F32 = jnp.float32
BF16 = jnp.bfloat16
WHOLE = pl.BlockSpec(memory_space=pltpu.VMEM)
SCALARS = pl.BlockSpec(memory_space=pltpu.SMEM)


def swap(value, axis, mask):
    return lax.ppermute(value, axis, [(i, i ^ mask) for i in range(lax.axis_size(axis))])


def call(kernel, out_shape, operands, in_specs, scratch=()):
    return pl.pallas_call(
        kernel,
        out_shape=out_shape,
        in_specs=in_specs,
        out_specs=jax.tree.map(lambda _: WHOLE, out_shape),
        scratch_shapes=list(scratch),
        compiler_params=pltpu.CompilerParams(vmem_limit_bytes=VMEM_LIMIT),
    )(*operands)


def shape(dims, dtype):
    return jax.ShapeDtypeStruct(tuple(dims), dtype)


def attend_kernel(C, E, heads, place, *refs):
    blocks, out_weight, mate_out, own_out, projected = refs[:C], *refs[C:]
    ctx, exp = place[0], place[1]
    rows = blocks[0].shape[0]
    seq = rows * C
    width = heads * HD
    half = HD // 2
    lower = (exp & 1) == 0

    def joined(start):
        own = jnp.concatenate([b[:, start : start + half] for b in blocks], axis=0)
        first = start + 2 * half
        mate = jnp.concatenate([b[:, first : first + half] for b in blocks], axis=0)
        both = jnp.concatenate([own, mate], axis=1)
        other = jnp.concatenate([mate, own], axis=1)
        return jnp.where(lower, both, other)

    keys = joined(width)
    values = joined(width + half)
    shift = rows.bit_length() - 1
    column = lax.broadcasted_iota(jnp.int32, (rows, seq), 1)
    key_position = ((column >> shift) ^ ctx) * rows + (column & (rows - 1))
    row = lax.broadcasted_iota(jnp.int32, (rows, seq), 0)
    parts = []
    for k in range(C):
        allowed = key_position <= (ctx ^ k) * rows + row
        block_parts = []
        for h in range(heads):
            q = blocks[k][:, h * HD : (h + 1) * HD]
            scores = lax.dot_general(
                q, keys, (((1,), (1,)), ((), ())), preferred_element_type=F32
            ) * (1.0 / math.sqrt(HD))
            scores = jnp.where(allowed, scores, -jnp.inf)
            top = jnp.max(scores, axis=1, keepdims=True)
            weights = jnp.exp(scores - top)
            total = jnp.sum(weights, axis=1, keepdims=True)
            high = weights.astype(BF16)
            low = (weights - high.astype(F32)).astype(BF16)
            summed = jnp.dot(high, values, preferred_element_type=F32) + jnp.dot(
                low, values, preferred_element_type=F32
            )
            block_parts.append((summed / total).astype(BF16))
        parts.append(jnp.concatenate(block_parts, axis=1))
    attended = jnp.concatenate(parts, axis=0)
    projected[...] = jnp.dot(attended, out_weight[...], preferred_element_type=F32)
    token_rows = mate_out.shape[2]
    for p in range(E):
        for k in range(C):
            start = pl.multiple_of((k * E + (exp ^ p)) * token_rows, token_rows)
            piece = projected[pl.ds(start, token_rows), :]
            if p & 1:
                mate_out[p >> 1, k] = piece.astype(BF16)
            else:
                own_out[p >> 1, k] = piece


def mate_sum_kernel(own, received, kept, *sent):
    kept[...] = own[0] + received[0].astype(F32)
    for p, out in enumerate(sent):
        out[...] = (own[p + 1] + received[p + 1].astype(F32)).astype(BF16)


def plane_sum_kernel(count, *refs):
    own, received, kept, sent = refs[0], refs[1 : 1 + count], refs[1 + count], refs[2 + count :]
    total = own[...]
    for piece in received:
        total = total + piece[...].astype(F32)
    kept[...] = total[0]
    for k, out in enumerate(sent):
        out[...] = total[k + 1].astype(BF16)


def norm_kernel(C, place, *refs):
    pieces, residual, gain, extra, hidden, rows_out = refs[:C], *refs[C:]
    ctx = place[0]
    cols = pieces[0].shape[1]
    features = residual.shape[1]
    for k in range(C):
        at = pl.ds(pl.multiple_of((ctx ^ k) * cols, 128), cols)
        hidden[:, at] = residual[:, at].astype(F32) + pieces[k][...].astype(F32)
    value = hidden[...]
    mean = jnp.sum(value, axis=1, keepdims=True) * (1.0 / features)
    centered = value - mean
    variance = jnp.sum(centered * centered, axis=1, keepdims=True) * (1.0 / features)
    normed = centered * lax.rsqrt(variance + 1e-05) * gain[...]
    rows_out[:, :features] = normed.astype(BF16)
    rows_out[:, features:] = extra[...]


def expert_kernel(E, groups, up_steps, place, *refs):
    packed = refs[: 2 * groups]
    gate, up, down = refs[2 * groups : 2 * groups + 3]
    outs = refs[2 * groups + 3 : 4 * groups + 3]
    rows, gate_sum, up_sum, activated, scale = refs[4 * groups + 3 :]
    step = pl.program_id(0)
    token_rows = packed[0].shape[1]
    features = rows.shape[1]
    depth = gate.shape[1]
    group_rows = packed[0].shape[0] * token_rows

    @pl.when(step == 0)
    def _():
        lane = lax.broadcasted_iota(jnp.int32, (group_rows, EXTRA), 1)
        wanted = ((lane & (E - 1)) == place[1]) & (lane < SPLIT * E)
        for g in range(2 * groups):
            at = slice(g * group_rows, (g + 1) * group_rows)
            value = packed[g][:, :, :features].astype(F32)
            rows[at, :] = value.reshape(group_rows, features).astype(BF16)
            tail = packed[g][:, :, features:].astype(F32).reshape(group_rows, EXTRA)
            scale[at, :] = jnp.sum(jnp.where(wanted, tail, 0.0), axis=1, keepdims=True)

    @pl.when(step < up_steps)
    def _():
        at = pl.ds(pl.multiple_of(step * depth, depth), depth)
        block = rows[:, at]
        gate_part = jnp.dot(block, gate[0], preferred_element_type=F32)
        up_part = jnp.dot(block, up[0], preferred_element_type=F32)

        @pl.when(step == 0)
        def _():
            gate_sum[...] = gate_part
            up_sum[...] = up_part

        @pl.when(step > 0)
        def _():
            gate_sum[...] += gate_part
            up_sum[...] += up_part

    @pl.when(step == up_steps)
    def _():
        value = gate_sum[...]
        activated[...] = (value / (1.0 + jnp.exp(-value)) * up_sum[...]).astype(BF16)

    @pl.when(step >= up_steps)
    def _():
        piece = jnp.dot(activated[...], down[0], preferred_element_type=F32) * scale[...]
        for g in range(2 * groups):
            part = piece[g * group_rows : (g + 1) * group_rows]
            outs[g][...] = part.reshape(-1, token_rows, part.shape[1]).astype(BF16)


def run_experts(place, packed, gate_weight, up_weight, down_weight, E):
    count = len(packed)
    pieces, token_rows, wide = packed[0].shape
    features = wide - EXTRA
    units = gate_weight.shape[2]
    total = count * pieces * token_rows
    depth = 512
    columns = 512
    up_steps = features // depth
    down_steps = features // columns
    last = up_steps - 1

    def column_block(i):
        return jnp.maximum(i - up_steps, 0)

    once = pl.Buffered(1)
    return pl.pallas_call(
        functools.partial(expert_kernel, E, count // 2, up_steps),
        out_shape=[shape((pieces, token_rows, features), BF16) for _ in packed],
        grid=(up_steps + down_steps,),
        in_specs=[SCALARS]
        + [
            pl.BlockSpec((pieces, token_rows, wide), lambda i: (0, 0, 0), pipeline_mode=once)
            for _ in packed
        ]
        + [
            pl.BlockSpec((1, depth, units), lambda i: (0, jnp.minimum(i, last), 0)),
            pl.BlockSpec((1, depth, units), lambda i: (0, jnp.minimum(i, last), 0)),
            pl.BlockSpec((1, units, columns), lambda i: (0, 0, column_block(i))),
        ],
        out_specs=[
            pl.BlockSpec((pieces, token_rows, columns), lambda i: (0, 0, column_block(i)))
            for _ in packed
        ],
        scratch_shapes=[
            pltpu.VMEM((total, features), BF16),
            pltpu.VMEM((total, units), F32),
            pltpu.VMEM((total, units), F32),
            pltpu.VMEM((total, units), BF16),
            pltpu.VMEM((total, 1), F32),
        ],
        compiler_params=pltpu.CompilerParams(
            vmem_limit_bytes=VMEM_LIMIT, dimension_semantics=("arbitrary",)
        ),
        cost_estimate=pl.CostEstimate(
            flops=6 * total * features * units,
            bytes_accessed=6 * features * units + 4 * total * features,
            transcendentals=total * units,
        ),
    )(place, *packed, gate_weight, up_weight, down_weight)


def group_sum_kernel(own, received, *outs):
    for i, out in enumerate(outs):
        out[...] = (own[i].astype(F32) + received[i].astype(F32)).astype(BF16)


def add(a, b):
    return (a.astype(F32) + b.astype(F32)).astype(BF16)


def on_device(
    queries,
    keys_values,
    residual,
    out_weight,
    norm_gain,
    routes,
    route_weight,
    gate_weight,
    up_weight,
    down_weight,
):
    C = lax.axis_size("ctx")
    E = lax.axis_size("exp")
    chips = E // 2
    chip_bits = list(range(1, E.bit_length() - 1))
    heads = queries.shape[1] // HD
    seq = queries.shape[0] * C
    token_rows, features = residual.shape
    cols = out_weight.shape[1]
    place = jnp.stack([lax.axis_index("ctx"), lax.axis_index("exp")]).astype(jnp.int32)

    own_kv = jnp.concatenate([keys_values[0], keys_values[1]], axis=1)
    bundle = jnp.concatenate([queries, own_kv, swap(own_kv, "exp", 1)], axis=1)
    blocks = [bundle] + [swap(bundle, "ctx", k) for k in range(1, C)]

    experts = jnp.arange(E, dtype=jnp.int32)
    left = jnp.sum(jnp.where(routes[:, :, None] == experts, route_weight[:, :, None], 0.0), axis=1)
    terms = []
    for _ in range(SPLIT):
        term = lax.reduce_precision(left, 8, 7)
        terms.append(term.astype(BF16))
        left = left - term
    extra = jnp.pad(jnp.concatenate(terms, axis=1), ((0, 0), (0, EXTRA - SPLIT * E)))

    mate_part, own_part = call(
        functools.partial(attend_kernel, C, E, heads),
        [
            shape((chips, C, token_rows, cols), BF16),
            shape((chips, C, token_rows, cols), F32),
        ],
        [place, *blocks, out_weight],
        [SCALARS] + [WHOLE] * (C + 1),
        [pltpu.VMEM((seq, cols), F32)],
    )

    kept, *sent = call(
        mate_sum_kernel,
        [shape((C, token_rows, cols), F32)] + [shape((C, token_rows, cols), BF16)] * (chips - 1),
        [own_part, swap(mate_part, "exp", 1)],
        [WHOLE, WHOLE],
    )
    received = [swap(piece, "exp", (p + 1) << 1) for p, piece in enumerate(sent)]
    kept, *sent = call(
        functools.partial(plane_sum_kernel, chips - 1),
        [shape((token_rows, cols), F32)] + [shape((token_rows, cols), BF16)] * (C - 1),
        [kept, *received],
        [WHOLE] * chips,
    )
    pieces = [kept] + [swap(piece, "ctx", k + 1) for k, piece in enumerate(sent)]
    hidden, rows = call(
        functools.partial(norm_kernel, C),
        [shape((token_rows, features), F32), shape((token_rows, features + EXTRA), BF16)],
        [place, *pieces, residual, norm_gain.reshape(1, -1), extra],
        [SCALARS] + [WHOLE] * (C + 3),
    )

    shards = [rows] + [swap(rows, "ctx", k) for k in range(1, C)]
    packed = []
    for g in range(C // 2):
        group = []
        for s in range(2):
            held = {0: shards[2 * g + s]}
            for bit in chip_bits if s else chip_bits[::-1]:
                for p in sorted(held):
                    held[p | 1 << (bit - 1)] = swap(held[p], "exp", 1 << bit)
            group += [held[p] for p in range(chips)]
        packed.append(jnp.stack(group))
    packed += [swap(group, "exp", 1) for group in packed]

    outs = run_experts(place, packed, gate_weight, up_weight, down_weight, E)

    count = C // 2
    shards = [None] * C
    for g in reversed(range(count)):
        received = swap(outs[count + g], "exp", 1)
        group = call(
            group_sum_kernel,
            [shape((token_rows, features), BF16)] * E,
            [outs[g], received],
            [WHOLE, WHOLE],
        )
        for s in range(2):
            held = dict(enumerate(group[s * chips : (s + 1) * chips]))
            for bit in chip_bits[::-1] if s else chip_bits:
                far = 1 << (bit - 1)
                for p in sorted(held):
                    if p & far:
                        held[p ^ far] = add(held[p ^ far], swap(held.pop(p), "exp", 1 << bit))
            shards[2 * g + s] = held[0]
    total = hidden
    for k, shard in enumerate(shards):
        total = total + (swap(shard, "ctx", k) if k else shard).astype(F32)
    return total.astype(BF16)


def solution(mesh):
    in_specs = (
        P("ctx", "exp"),
        P(None, "ctx", "exp"),
        P(("ctx", "exp"), None),
        P("exp", "ctx"),
        P(),
        P(("ctx", "exp"), None),
        P(("ctx", "exp"), None),
        P("exp", None, "ctx"),
        P("exp", None, "ctx"),
        P("exp", "ctx", None),
    )
    out_specs = P(("ctx", "exp"), None)
    return jax.shard_map(
        on_device, mesh=mesh, in_specs=in_specs, out_specs=out_specs, check_vma=False
    )
```

time: 294 us -> 203 us (0.69)
  waiting for transfers between devices: 155 us -> 40.4 us
  blocking collectives: 77.8 us -> 0 us
  Pallas kernels: 0 us -> 49.9 us
  local copies, waits for them, and re-layouts: 1.18 us -> 50.8 us
  starting transfers between devices: 0.54 us -> 48.2 us
  matrix products: 41.7 us -> 0 us
  between operations: 13.2 us -> 0.26 us
  other arithmetic: 3.99 us -> 11.1 us
    reduce_scatter x2 -> x0, waiting for transfers between devices: 137 us -> none  [the longest x1 100 us: on_device(): lax.psum_scatter(weighted, ('ctx', 'exp'), scatter_dimension=0, tiled=True)]
    all_gather x3 -> x0, blocking collectives: 67.4 us -> none  [the longest x1 38.7 us: on_device(): lax.all_gather(own_weights, ('ctx', 'exp'), axis=0, tiled=True)]
    unnamed x10 -> x52, local copies, waits for them, and re-layouts: 0.03 us -> 50 us
    pallas_call x0 -> x7, Pallas kernels: none -> 49.9 us  [the longest x1 35.8 us: run_experts(): pl.pallas_call(functools.partial(expert_kernel, E, count // 2, up_steps),...]
    ppermute x1 -> x45, starting transfers between devices: 0.45 us -> 48.2 us  [swap(): lax.ppermute(value, axis, [(i, i ^ mask) for i in range(lax.axis_size(axi...]
    dot_general x5 -> x0, matrix products: 41.7 us -> none  [the longest x1 31.2 us: on_device(): jnp.dot(activated, down_weight[0], preferred_element_type=jnp.float32)]
    ppermute x1 -> x45, waiting for transfers between devices: 0.01 us -> 40.4 us  [swap(): lax.ppermute(value, axis, [(i, i ^ mask) for i in range(lax.axis_size(axi...]
    all_gather x1 -> x0, waiting for transfers between devices: 18 us -> none  [on_device(): rows = lax.all_gather(normed, ('ctx', 'exp'), axis=0, tiled=True)]
  transfers between devices with their start and end apart: 4 -> 45, of which waited for: 3 -> 21; matrix products, arithmetic and copies ran while one was open for 0% -> 26% of each run, Pallas kernels for 0% -> 2%
where the time goes in v2:
time: 203 us; the launch traced here: 201 us
  local copies, waits for them, and re-layouts  50.8 us (25%)
  Pallas kernels  49.9 us (25%)
  starting transfers between devices  48.2 us (24%)
  waiting for transfers between devices  40.4 us (20%)
  other arithmetic  11.1 us (5%)
    unnamed x52, local copies, waits for them, and re-layouts  50 us
    ppermute x45, starting transfers between devices, swap(): lax.ppermute(value, axis, [(i, i ^ mask) for i in range(lax.axis_size(axi...  48.2 us
    ppermute x45, waiting for transfers between devices, swap(): lax.ppermute(value, axis, [(i, i ^ mask) for i in range(lax.axis_size(axi...  40.4 us
    pallas_call x1, Pallas kernels, run_experts(): pl.pallas_call(functools.partial(expert_kernel, E, count // 2, up_steps),...  35.8 us
    pallas_call x6, Pallas kernels, call(): pl.pallas_call(kernel, out_shape=out_shape, in_specs=in_specs, out_specs=...  14.2 us
    convert_element_type x7, other arithmetic, add(): return (a.astype(F32) + b.astype(F32)).astype(BF16)  6.47 us
  transfers between devices with their start and end apart: 45, of which 21 were waited for; matrix products, arithmetic and copies ran while one was open for 26% of the time, Pallas kernels for 2%

profile of v2, /device:TPU:0, one launch (start us, length us, event | category | flops | bytes accessed | tf_op | source)
XLA Modules:
  0.0 200.7 jit_solution(12022136378022970545)
XLA Ops:
  3.0 5.0 %collective-permute-start.3 = (bf16[64,640]{1,0:T(8,128)(2,1)S(1)}, bf16[64,640]{1,0:T(8,128)(2,1)S(1)}, u32[]{:S(2)}, u32[]{:S(2)}) collective-permute-start(bf16[64,640]{1,0:T(8,128)(2,1)S(1)} %pad_maximum_fusion.refs_0_), channel_id=1, source_target_pairs={{0,24},{8,16},{16,8},{24,0},{1,25},{9,17},{17,9},{25,1},{2,26},{10... | collective-permute-start | bytes 245768 | tf_op jit(solution)/shard_map/ppermute | solution.py:22
  9.3 2.1 %collective-permute-done.3.refs_3_ = bf16[64,640]{1,0:T(8,128)(2,1)S(1)} collective-permute-done((bf16[64,640]{1,0:T(8,128)(2,1)S(1)}, bf16[64,640]{1,0:T(8,128)(2,1)S(1)}, u32[]{:S(2)}, u32[]{:S(2)}) %collective-permute-start.3) | collective-permute-done | bytes 81952 | tf_op jit(solution)/shard_map/ppermute | solution.py:22
  11.4 3.8 %collective-permute-done.2.refs_2_ = bf16[64,640]{1,0:T(8,128)(2,1)S(1)} collective-permute-done((bf16[64,640]{1,0:T(8,128)(2,1)S(1)}, bf16[64,640]{1,0:T(8,128)(2,1)S(1)}, u32[]{:S(2)}, u32[]{:S(2)}) %collective-permute-start.2) | collective-permute-done | bytes 81952 | tf_op jit(solution)/shard_map/ppermute | solution.py:22
  16.5 3.8 %shard_map.100 = (bf16[4,4,8,1536]{3,2,1,0:T(8,128)(2,1)}, f32[4,4,8,1536]{3,2,1,0:T(8,128)}) custom-call(s32[2]{0:T(128)} %pad_add_fusion.place, bf16[64,640]{1,0:T(8,128)(2,1)} %copy-done.7, bf16[64,640]{1,0:T(8,128)(2,1)} %copy-done.14, bf16[64,640]{1,0:T(8,128)(2,1)} %copy-done.13, bf16[64,640]{1,0:T(8,128)(2,1)} %copy-done.12, bf16[384,1536]{1,0:T(8,128)(2,1)} %refs_4_.3), custom_call_target="tpu_custom_call" | custom-call | tf_op jit(solution)/shard_map/pallas_call | solution.py:26
  23.0 2.0 %shard_map.101 = (f32[4,8,1536]{2,1,0:T(8,128)}, bf16[4,8,1536]{2,1,0:T(8,128)(2,1)}, bf16[4,8,1536]{2,1,0:T(8,128)(2,1)}, bf16[4,8,1536]{2,1,0:T(8,128)(2,1)}) custom-call(f32[4,4,8,1536]{3,2,1,0:T(8,128)} %get-tuple-element.37.own, bf16[4,4,8,1536]{3,2,1,0:T(8,128)(2,1)} %copy-done.6), custom_call_target="tpu_custom_call" | custom-call | tf_op jit(solution)/shard_map/pallas_call | solution.py:26
  25.0 1.5 collective-permute-start.5
  26.5 1.5 collective-permute-start.6
  28.5 1.5 collective-permute-done.5.refs_1_
  30.1 2.5 %collective-permute-done.6.refs_2_ = bf16[4,8,1536]{2,1,0:T(8,128)(2,1)S(1)} collective-permute-done((bf16[4,8,1536]{2,1,0:T(8,128)(2,1)}, bf16[4,8,1536]{2,1,0:T(8,128)(2,1)S(1)}, u32[]{:S(2)}, u32[]{:S(2)}) %collective-permute-start.6) | collective-permute-done | bytes 98336 | tf_op jit(solution)/shard_map/ppermute | solution.py:22
  34.4 1.8 shard_map.102
  36.4 2.8 %collective-permute-start.9 = (bf16[8,1536]{1,0:T(8,128)(2,1)}, bf16[8,1536]{1,0:T(8,128)(2,1)S(1)}, u32[]{:S(2)}, u32[]{:S(2)}) collective-permute-start(bf16[8,1536]{1,0:T(8,128)(2,1)} %get-tuple-element.45), channel_id=1, source_target_pairs={{0,16},{8,24},{16,0},{24,8},{1,17},{9,25},{17,1},{25,9},{2,18},{10... | collective-permute-start | bytes 73736 | tf_op jit(solution)/shard_map/ppermute | solution.py:22
  41.4 3.7 %collective-permute-done.10.refs_3_ = bf16[8,1536]{1,0:T(8,128)(2,1)S(1)} collective-permute-done((bf16[8,1536]{1,0:T(8,128)(2,1)}, bf16[8,1536]{1,0:T(8,128)(2,1)S(1)}, u32[]{:S(2)}, u32[]{:S(2)}) %collective-permute-start.10) | collective-permute-done | bytes 24608 | tf_op jit(solution)/shard_map/ppermute | solution.py:22
  45.7 2.0 shard_map.103
  49.0 3.0 %collective-permute-start.14 = (bf16[8,6272]{1,0:T(8,128)(2,1)}, bf16[8,6272]{1,0:T(8,128)(2,1)S(1)}, u32[]{:S(2)}, u32[]{:S(2)}) collective-permute-start(bf16[8,6272]{1,0:T(8,128)(2,1)} %get-tuple-element.48), channel_id=1, source_target_pairs={{0,8},{8,0},{16,24},{24,16},{1,9},{9,1},{17,25},{25,17},{2,10},{10... | collective-permute-start | bytes 301064 | tf_op jit(solution)/shard_map/ppermute | solution.py:22
  60.8 3.0 %collective-permute-done.19 = bf16[8,6272]{1,0:T(8,128)(2,1)S(1)} collective-permute-done((bf16[8,6272]{1,0:T(8,128)(2,1)S(1)}, bf16[8,6272]{1,0:T(8,128)(2,1)S(1)}, u32[]{:S(2)}, u32[]{:S(2)}) %collective-permute-start.19) | collective-permute-done | bytes 100384 | tf_op jit(solution)/shard_map/ppermute | solution.py:22
  66.8 2.4 %collective-permute-done.15 = bf16[8,6272]{1,0:T(8,128)(2,1)S(1)} collective-permute-done((bf16[8,6272]{1,0:T(8,128)(2,1)S(1)}, bf16[8,6272]{1,0:T(8,128)(2,1)S(1)}, u32[]{:S(2)}, u32[]{:S(2)}) %collective-permute-start.15) | collective-permute-done | bytes 100384 | tf_op jit(solution)/shard_map/ppermute | solution.py:22
  71.6 3.5 %collective-permute-done.17 = bf16[8,6272]{1,0:T(8,128)(2,1)S(1)} collective-permute-done((bf16[8,6272]{1,0:T(8,128)(2,1)S(1)}, bf16[8,6272]{1,0:T(8,128)(2,1)S(1)}, u32[]{:S(2)}, u32[]{:S(2)}) %collective-permute-start.17) | collective-permute-done | bytes 100384 | tf_op jit(solution)/shard_map/ppermute | solution.py:22
  75.9 21.1 %copy.15.refs_4_ = bf16[1,6144,1344]{2,1,0:T(8,128)(2,1)} copy(bf16[1,6144,1344]{1,2,0:T(8,128)(2,1)} %param.17) | data formatting | bytes 33030144 | tf_op args[7]
  97.1 20.8 %copy.16.refs_5_ = bf16[1,6144,1344]{2,1,0:T(8,128)(2,1)} copy(bf16[1,6144,1344]{1,2,0:T(8,128)(2,1)} %param.18) | data formatting | bytes 33030144 | tf_op args[8]
  119.7 35.8 %shard_map.104 = (bf16[8,8,6144]{2,1,0:T(8,128)(2,1)}, bf16[8,8,6144]{2,1,0:T(8,128)(2,1)}, bf16[8,8,6144]{2,1,0:T(8,128)(2,1)}, bf16[8,8,6144]{2,1,0:T(8,128)(2,1)}) custom-call(s32[2]{0:T(128)} %pad_add_fusion.place, bf16[8,8,6272]{2,1,0:T(8,128)(2,1)} %copy-done.1, bf16[8,8,6272]{2,1,0:T(8,128)(2,1)} %copy-done, bf16[8,8,6272]{2,1,0:T(8,128)(2,1)} %copy-done.2, ...), custom_call_target="tpu_custom_call" | custom-call | flops 12683575296 | bytes 55836672 | tf_op jit(solution)/shard_map/pallas_call | solution.py:197
  156.1 2.0 collective-permute-done.28.received
  159.0 2.3 %shard_map.105 = (bf16[8,6144]{1,0:T(8,128)(2,1)}, bf16[8,6144]{1,0:T(8,128)(2,1)}, bf16[8,6144]{1,0:T(8,128)(2,1)}, bf16[8,6144]{1,0:T(8,128)(2,1)}, bf16[8,614...) custom-call(bf16[8,8,6144]{2,1,0:T(8,128)(2,1)} %get-tuple-element.49.own, ...), custom_call_target="tpu_custom_call" | custom-call | tf_op jit(solution)/shard_map/pallas_call | solution.py:26
  161.9 1.4 collective-permute-start.29
  166.3 2.3 %shard_map.106 = (bf16[8,6144]{1,0:T(8,128)(2,1)}, bf16[8,6144]{1,0:T(8,128)(2,1)}, bf16[8,6144]{1,0:T(8,128)(2,1)}, bf16[8,6144]{1,0:T(8,128)(2,1)}, bf16[8,614...) custom-call(bf16[8,8,6144]{2,1,0:T(8,128)(2,1)} %get-tuple-element.59.own, ...), custom_call_target="tpu_custom_call" | custom-call | tf_op jit(solution)/shard_map/pallas_call | solution.py:26
  169.1 1.4 collective-permute-start.38
  176.6 2.9 %collective-permute-done.42 = bf16[8,6144]{1,0:T(8,128)(2,1)S(1)} collective-permute-done((bf16[8,6144]{1,0:T(8,128)(2,1)}, bf16[8,6144]{1,0:T(8,128)(2,1)S(1)}, u32[]{:S(2)}, u32[]{:S(2)}) %collective-permute-start.42) | collective-permute-done | bytes 98336 | tf_op jit(solution)/shard_map/ppermute | solution.py:22
  182.3 1.8 collective-permute-done.34
  186.9 1.8 collective-permute-done.39
  192.5 2.7 %collective-permute-start.44 = (bf16[8,6144]{1,0:T(8,128)(2,1)S(1)}, bf16[8,6144]{1,0:T(8,128)(2,1)S(1)}, u32[]{:S(2)}, u32[]{:S(2)}) collective-permute-start(bf16[8,6144]{1,0:T(8,128)(2,1)S(1)} %add_convert_fusion.1), channel_id=1, source_target_pairs={{0,24},{8,16},{16,8},{24,0},{1,25},{9,17},{17,9},{25,1},{2,26},{10... | collective-permute-start | bytes 294920 | tf_op jit(solution)/shard_map/ppermute | solution.py:22
  195.1 2.3 %collective-permute-done.40 = bf16[8,6144]{1,0:T(8,128)(2,1)S(1)} collective-permute-done((bf16[8,6144]{1,0:T(8,128)(2,1)S(1)}, bf16[8,6144]{1,0:T(8,128)(2,1)S(1)}, u32[]{:S(2)}, u32[]{:S(2)}) %collective-permute-start.40) | collective-permute-done | bytes 98336 | tf_op jit(solution)/shard_map/ppermute | solution.py:22
  197.5 1.6 collective-permute-done.44
  199.1 1.6 add_convert_fusion
  (134 shorter events, 52.7 us)
Async XLA Ops:
  3.0 8.4 %collective-permute-start.3 = (bf16[64,640]{1,0:T(8,128)(2,1)S(1)}, bf16[64,640]{1,0:T(8,128)(2,1)S(1)}, u32[]{:S(2)}, u32[]{:S(2)}) collective-permute-start(bf16[64,640]{1,0:T(8,128)(2,1)S(1)} %pad_maximum_fusion.refs_0_), channel_id=1, source_target_pairs={{0,24},{8,16},{16,8},{24,0},{1,25},{9,17},{17,9},{25,1},{2,26},{10... | collective-permute-start | bytes 245768 | tf_op jit(solution)/shard_map/ppermute | solution.py:22
  8.0 7.2 %collective-permute-start.2 = (bf16[64,640]{1,0:T(8,128)(2,1)S(1)}, bf16[64,640]{1,0:T(8,128)(2,1)S(1)}, u32[]{:S(2)}, u32[]{:S(2)}) collective-permute-start(bf16[64,640]{1,0:T(8,128)(2,1)S(1)} %pad_maximum_fusion.refs_0_), channel_id=1, source_target_pairs={{0,16},{8,24},{16,0},{24,8},{1,17},{9,25},{17,1},{25,9},{2,18},{10... | collective-permute-start | bytes 245768 | tf_op jit(solution)/shard_map/ppermute | solution.py:22
  8.0 7.2 %collective-permute-start.1 = (bf16[64,640]{1,0:T(8,128)(2,1)S(1)}, bf16[64,640]{1,0:T(8,128)(2,1)S(1)}, u32[]{:S(2)}, u32[]{:S(2)}) collective-permute-start(bf16[64,640]{1,0:T(8,128)(2,1)S(1)} %pad_maximum_fusion.refs_0_), channel_id=1, source_target_pairs={{0,8},{8,0},{16,24},{24,16},{1,9},{9,1},{17,25},{25,17},{2,10},{10... | collective-permute-start | bytes 245768 | tf_op jit(solution)/shard_map/ppermute | solution.py:22
  26.5 6.1 %collective-permute-start.6 = (bf16[4,8,1536]{2,1,0:T(8,128)(2,1)}, bf16[4,8,1536]{2,1,0:T(8,128)(2,1)S(1)}, u32[]{:S(2)}, u32[]{:S(2)}) collective-permute-start(bf16[4,8,1536]{2,1,0:T(8,128)(2,1)} %get-tuple-element.41), channel_id=1, source_target_pairs={{0,4},{1,5},{2,6},{3,7},{4,0},{5,1},{6,2},{7,3},{8,12},{9,13},{10,... | collective-permute-start | bytes 294920 | tf_op jit(solution)/shard_map/ppermute | solution.py:22
  28.1 5.7 %collective-permute-start.7 = (bf16[4,8,1536]{2,1,0:T(8,128)(2,1)}, bf16[4,8,1536]{2,1,0:T(8,128)(2,1)S(1)}, u32[]{:S(2)}, u32[]{:S(2)}) collective-permute-start(bf16[4,8,1536]{2,1,0:T(8,128)(2,1)} %get-tuple-element.42), channel_id=1, source_target_pairs={{0,6},{1,7},{2,4},{3,5},{4,2},{5,3},{6,0},{7,1},{8,14},{9,15},{10,... | collective-permute-start | bytes 294920 | tf_op jit(solution)/shard_map/ppermute | solution.py:22
  39.2 5.8 %collective-permute-start.10 = (bf16[8,1536]{1,0:T(8,128)(2,1)}, bf16[8,1536]{1,0:T(8,128)(2,1)S(1)}, u32[]{:S(2)}, u32[]{:S(2)}) collective-permute-start(bf16[8,1536]{1,0:T(8,128)(2,1)} %get-tuple-element.46), channel_id=1, source_target_pairs={{0,24},{8,16},{16,8},{24,0},{1,25},{9,17},{17,9},{25,1},{2,26},{10... | collective-permute-start | bytes 73736 | tf_op jit(solution)/shard_map/ppermute | solution.py:22
  47.6 7.1 %collective-permute-start.22 = (bf16[8,6272]{1,0:T(8,128)(2,1)}, bf16[8,6272]{1,0:T(8,128)(2,1)S(1)}, u32[]{:S(2)}, u32[]{:S(2)}) collective-permute-start(bf16[8,6272]{1,0:T(8,128)(2,1)} %get-tuple-element.48), channel_id=1, source_target_pairs={{0,24},{8,16},{16,8},{24,0},{1,25},{9,17},{17,9},{25,1},{2,26},{10... | collective-permute-start | bytes 301064 | tf_op jit(solution)/shard_map/ppermute | solution.py:22
  49.0 7.5 %collective-permute-start.18 = (bf16[8,6272]{1,0:T(8,128)(2,1)}, bf16[8,6272]{1,0:T(8,128)(2,1)S(1)}, u32[]{:S(2)}, u32[]{:S(2)}) collective-permute-start(bf16[8,6272]{1,0:T(8,128)(2,1)} %get-tuple-element.48), channel_id=1, source_target_pairs={{0,16},{8,24},{16,0},{24,8},{1,17},{9,25},{17,1},{25,9},{2,18},{10... | collective-permute-start | bytes 301064 | tf_op jit(solution)/shard_map/ppermute | solution.py:22
  49.0 10.1 %collective-permute-start.14 = (bf16[8,6272]{1,0:T(8,128)(2,1)}, bf16[8,6272]{1,0:T(8,128)(2,1)S(1)}, u32[]{:S(2)}, u32[]{:S(2)}) collective-permute-start(bf16[8,6272]{1,0:T(8,128)(2,1)} %get-tuple-element.48), channel_id=1, source_target_pairs={{0,8},{8,0},{16,24},{24,16},{1,9},{9,1},{17,25},{25,17},{2,10},{10... | collective-permute-start | bytes 301064 | tf_op jit(solution)/shard_map/ppermute | solution.py:22
  52.0 8.0 %collective-permute-start.12 = (bf16[8,6272]{1,0:T(8,128)(2,1)}, bf16[8,6272]{1,0:T(8,128)(2,1)S(1)}, u32[]{:S(2)}, u32[]{:S(2)}) collective-permute-start(bf16[8,6272]{1,0:T(8,128)(2,1)} %get-tuple-element.48), channel_id=1, source_target_pairs={{0,4},{1,5},{2,6},{3,7},{4,0},{5,1},{6,2},{7,3},{8,12},{9,13},{10,... | collective-permute-start | bytes 301064 | tf_op jit(solution)/shard_map/ppermute | solution.py:22
  54.7 20.6 %collective-permute-start.24 = (bf16[8,6272]{1,0:T(8,128)(2,1)S(1)}, bf16[8,6272]{1,0:T(8,128)(2,1)S(1)}, u32[]{:S(2)}, u32[]{:S(2)}) collective-permute-start(bf16[8,6272]{1,0:T(8,128)(2,1)S(1)} %collective-permute-done.22), channel_id=1, source_target_pairs={{0,4},{1,5},{2,6},{3,7},{4,0},{5,1},{6,2},{7,3},{8,12},{9,13},{10,... | collective-permute-start | bytes 301064 | tf_op jit(solution)/shard_map/ppermute | solution.py:22
  56.5 9.4 %collective-permute-start.23 = (bf16[8,6272]{1,0:T(8,128)(2,1)S(1)}, bf16[8,6272]{1,0:T(8,128)(2,1)S(1)}, u32[]{:S(2)}, u32[]{:S(2)}) collective-permute-start(bf16[8,6272]{1,0:T(8,128)(2,1)S(1)} %collective-permute-done.22), channel_id=1, source_target_pairs={{0,2},{1,3},{2,0},{3,1},{4,6},{5,7},{6,4},{7,5},{8,10},{9,11},{10,... | collective-permute-start | bytes 301064 | tf_op jit(solution)/shard_map/ppermute | solution.py:22
  58.3 6.3 %collective-permute-start.20 = (bf16[8,6272]{1,0:T(8,128)(2,1)S(1)}, bf16[8,6272]{1,0:T(8,128)(2,1)S(1)}, u32[]{:S(2)}, u32[]{:S(2)}) collective-permute-start(bf16[8,6272]{1,0:T(8,128)(2,1)S(1)} %collective-permute-done.18), channel_id=1, source_target_pairs={{0,4},{1,5},{2,6},{3,7},{4,0},{5,1},{6,2},{7,3},{8,12},{9,13},{10,... | collective-permute-start | bytes 301064 | tf_op jit(solution)/shard_map/ppermute | solution.py:22
  60.0 11.6 %collective-permute-start.16 = (bf16[8,6272]{1,0:T(8,128)(2,1)S(1)}, bf16[8,6272]{1,0:T(8,128)(2,1)S(1)}, u32[]{:S(2)}, u32[]{:S(2)}) collective-permute-start(bf16[8,6272]{1,0:T(8,128)(2,1)S(1)} %collective-permute-done.14), channel_id=1, source_target_pairs={{0,4},{1,5},{2,6},{3,7},{4,0},{5,1},{6,2},{7,3},{8,12},{9,13},{10,... | collective-permute-start | bytes 301064 | tf_op jit(solution)/shard_map/ppermute | solution.py:22
  63.7 5.5 %collective-permute-start.15 = (bf16[8,6272]{1,0:T(8,128)(2,1)S(1)}, bf16[8,6272]{1,0:T(8,128)(2,1)S(1)}, u32[]{:S(2)}, u32[]{:S(2)}) collective-permute-start(bf16[8,6272]{1,0:T(8,128)(2,1)S(1)} %collective-permute-done.14), channel_id=1, source_target_pairs={{0,2},{1,3},{2,0},{3,1},{4,6},{5,7},{6,4},{7,5},{8,10},{9,11},{10,... | collective-permute-start | bytes 301064 | tf_op jit(solution)/shard_map/ppermute | solution.py:22
  64.6 5.9 %collective-permute-start.13 = (bf16[8,6272]{1,0:T(8,128)(2,1)S(1)}, bf16[8,6272]{1,0:T(8,128)(2,1)S(1)}, u32[]{:S(2)}, u32[]{:S(2)}) collective-permute-start(bf16[8,6272]{1,0:T(8,128)(2,1)S(1)} %collective-permute-done.12), channel_id=1, source_target_pairs={{0,2},{1,3},{2,0},{3,1},{4,6},{5,7},{6,4},{7,5},{8,10},{9,11},{10,... | collective-permute-start | bytes 301064 | tf_op jit(solution)/shard_map/ppermute | solution.py:22
  65.9 9.4 %collective-permute-start.21 = (bf16[8,6272]{1,0:T(8,128)(2,1)S(1)}, bf16[8,6272]{1,0:T(8,128)(2,1)S(1)}, u32[]{:S(2)}, u32[]{:S(2)}) collective-permute-start(bf16[8,6272]{1,0:T(8,128)(2,1)S(1)} %collective-permute-done.20), channel_id=1, source_target_pairs={{0,2},{1,3},{2,0},{3,1},{4,6},{5,7},{6,4},{7,5},{8,10},{9,11},{10,... | collective-permute-start | bytes 301064 | tf_op jit(solution)/shard_map/ppermute | solution.py:22
  69.2 6.1 %collective-permute-start.25 = (bf16[8,6272]{1,0:T(8,128)(2,1)S(1)}, bf16[8,6272]{1,0:T(8,128)(2,1)S(1)}, u32[]{:S(2)}, u32[]{:S(2)}) collective-permute-start(bf16[8,6272]{1,0:T(8,128)(2,1)S(1)} %collective-permute-done.23), channel_id=1, source_target_pairs={{0,4},{1,5},{2,6},{3,7},{4,0},{5,1},{6,2},{7,3},{8,12},{9,13},{10,... | collective-permute-start | bytes 301064 | tf_op jit(solution)/shard_map/ppermute | solution.py:22
  75.2 42.8 %collective-permute-start.26 = (bf16[8,8,6272]{2,1,0:T(8,128)(2,1)S(1)}, bf16[8,8,6272]{2,1,0:T(8,128)(2,1)S(1)}, u32[]{:S(2)}, u32[]{:S(2)}) collective-permute-start(bf16[8,8,6272]{2,1,0:T(8,128)(2,1)S(1)} %bitcast_dynamic-update-slice_fusion.8.refs_0_), channel_id=1, source_target_pairs={{0,1},{1,0},{2,3},{3,2},{4,5},{5,4},{6,7},{7,6},{8,9},{9,8},{10,11... | collective-permute-start | bytes 2408456 | tf_op jit(solution)/shard_map/ppermute | solution.py:22
  75.4 42.6 %collective-permute-start.27 = (bf16[8,8,6272]{2,1,0:T(8,128)(2,1)S(1)}, bf16[8,8,6272]{2,1,0:T(8,128)(2,1)S(1)}, u32[]{:S(2)}, u32[]{:S(2)}) collective-permute-start(bf16[8,8,6272]{2,1,0:T(8,128)(2,1)S(1)} %bitcast_dynamic-update-slice_fusion.refs_1_), channel_id=1, source_target_pairs={{0,1},{1,0},{2,3},{3,2},{4,5},{5,4},{6,7},{7,6},{8,9},{9,8},{10,11... | collective-permute-start | bytes 2408456 | tf_op jit(solution)/shard_map/ppermute | solution.py:22
  155.8 9.5 %collective-permute-start.36 = (bf16[8,8,6144]{2,1,0:T(8,128)(2,1)}, bf16[8,8,6144]{2,1,0:T(8,128)(2,1)S(1)}, u32[]{:S(2)}, u32[]{:S(2)}) collective-permute-start(bf16[8,8,6144]{2,1,0:T(8,128)(2,1)} %get-tuple-element.60), channel_id=1, source_target_pairs={{0,1},{1,0},{2,3},{3,2},{4,5},{5,4},{6,7},{7,6},{8,9},{9,8},{10,11... | collective-permute-start | bytes 2359304 | tf_op jit(solution)/shard_map/ppermute | solution.py:22
  161.3 7.8 %collective-permute-start.30 = (bf16[8,6144]{1,0:T(8,128)(2,1)}, bf16[8,6144]{1,0:T(8,128)(2,1)S(1)}, u32[]{:S(2)}, u32[]{:S(2)}) collective-permute-start(bf16[8,6144]{1,0:T(8,128)(2,1)} %get-tuple-element.54), channel_id=1, source_target_pairs={{0,2},{1,3},{2,0},{3,1},{4,6},{5,7},{6,4},{7,5},{8,10},{9,11},{10,... | collective-permute-start | bytes 294920 | tf_op jit(solution)/shard_map/ppermute | solution.py:22
  161.9 33.3 %collective-permute-start.29 = (bf16[8,6144]{1,0:T(8,128)(2,1)}, bf16[8,6144]{1,0:T(8,128)(2,1)S(1)}, u32[]{:S(2)}, u32[]{:S(2)}) collective-permute-start(bf16[8,6144]{1,0:T(8,128)(2,1)} %get-tuple-element.52), channel_id=1, source_target_pairs={{0,2},{1,3},{2,0},{3,1},{4,6},{5,7},{6,4},{7,5},{8,10},{9,11},{10,... | collective-permute-start | bytes 294920 | tf_op jit(solution)/shard_map/ppermute | solution.py:22
  163.3 17.8 %collective-permute-start.32 = (bf16[8,6144]{1,0:T(8,128)(2,1)}, bf16[8,6144]{1,0:T(8,128)(2,1)S(1)}, u32[]{:S(2)}, u32[]{:S(2)}) collective-permute-start(bf16[8,6144]{1,0:T(8,128)(2,1)} %get-tuple-element.56), channel_id=1, source_target_pairs={{0,4},{1,5},{2,6},{3,7},{4,0},{5,1},{6,2},{7,3},{8,12},{9,13},{10,... | collective-permute-start | bytes 294920 | tf_op jit(solution)/shard_map/ppermute | solution.py:22
  164.4 7.1 %collective-permute-start.33 = (bf16[8,6144]{1,0:T(8,128)(2,1)}, bf16[8,6144]{1,0:T(8,128)(2,1)S(1)}, u32[]{:S(2)}, u32[]{:S(2)}) collective-permute-start(bf16[8,6144]{1,0:T(8,128)(2,1)} %get-tuple-element.58), channel_id=1, source_target_pairs={{0,4},{1,5},{2,6},{3,7},{4,0},{5,1},{6,2},{7,3},{8,12},{9,13},{10,... | collective-permute-start | bytes 294920 | tf_op jit(solution)/shard_map/ppermute | solution.py:22
  168.5 17.6 %collective-permute-start.37 = (bf16[8,6144]{1,0:T(8,128)(2,1)}, bf16[8,6144]{1,0:T(8,128)(2,1)S(1)}, u32[]{:S(2)}, u32[]{:S(2)}) collective-permute-start(bf16[8,6144]{1,0:T(8,128)(2,1)} %get-tuple-element.62), channel_id=1, source_target_pairs={{0,2},{1,3},{2,0},{3,1},{4,6},{5,7},{6,4},{7,5},{8,10},{9,11},{10,... | collective-permute-start | bytes 294920 | tf_op jit(solution)/shard_map/ppermute | solution.py:22
  169.1 5.5 %collective-permute-start.38 = (bf16[8,6144]{1,0:T(8,128)(2,1)}, bf16[8,6144]{1,0:T(8,128)(2,1)S(1)}, u32[]{:S(2)}, u32[]{:S(2)}) collective-permute-start(bf16[8,6144]{1,0:T(8,128)(2,1)} %get-tuple-element.64), channel_id=1, source_target_pairs={{0,2},{1,3},{2,0},{3,1},{4,6},{5,7},{6,4},{7,5},{8,10},{9,11},{10,... | collective-permute-start | bytes 294920 | tf_op jit(solution)/shard_map/ppermute | solution.py:22
  171.5 19.3 %collective-permute-start.41 = (bf16[8,6144]{1,0:T(8,128)(2,1)}, bf16[8,6144]{1,0:T(8,128)(2,1)S(1)}, u32[]{:S(2)}, u32[]{:S(2)}) collective-permute-start(bf16[8,6144]{1,0:T(8,128)(2,1)} %get-tuple-element.66), channel_id=1, source_target_pairs={{0,4},{1,5},{2,6},{3,7},{4,0},{5,1},{6,2},{7,3},{8,12},{9,13},{10,... | collective-permute-start | bytes 294920 | tf_op jit(solution)/shard_map/ppermute | solution.py:22
  181.1 14.0 %collective-permute-start.31 = (bf16[8,6144]{1,0:T(8,128)(2,1)S(1)}, bf16[8,6144]{1,0:T(8,128)(2,1)S(1)}, u32[]{:S(2)}, u32[]{:S(2)}) collective-permute-start(bf16[8,6144]{1,0:T(8,128)(2,1)S(1)} %add_convert_fusion.11), channel_id=1, source_target_pairs={{0,4},{1,5},{2,6},{3,7},{4,0},{5,1},{6,2},{7,3},{8,12},{9,13},{10,... | collective-permute-start | bytes 294920 | tf_op jit(solution)/shard_map/ppermute | solution.py:22
  188.7 6.4 %collective-permute-start.35 = (bf16[8,6144]{1,0:T(8,128)(2,1)S(1)}, bf16[8,6144]{1,0:T(8,128)(2,1)S(1)}, u32[]{:S(2)}, u32[]{:S(2)}) collective-permute-start(bf16[8,6144]{1,0:T(8,128)(2,1)S(1)} %add_convert_fusion.7), channel_id=1, source_target_pairs={{0,8},{8,0},{16,24},{24,16},{1,9},{9,1},{17,25},{25,17},{2,10},{10... | collective-permute-start | bytes 294920 | tf_op jit(solution)/shard_map/ppermute | solution.py:22
  190.8 6.6 %collective-permute-start.40 = (bf16[8,6144]{1,0:T(8,128)(2,1)S(1)}, bf16[8,6144]{1,0:T(8,128)(2,1)S(1)}, u32[]{:S(2)}, u32[]{:S(2)}) collective-permute-start(bf16[8,6144]{1,0:T(8,128)(2,1)S(1)} %add_convert_fusion.4), channel_id=1, source_target_pairs={{0,16},{8,24},{16,0},{24,8},{1,17},{9,25},{17,1},{25,9},{2,18},{10... | collective-permute-start | bytes 294920 | tf_op jit(solution)/shard_map/ppermute | solution.py:22
  192.5 6.6 %collective-permute-start.44 = (bf16[8,6144]{1,0:T(8,128)(2,1)S(1)}, bf16[8,6144]{1,0:T(8,128)(2,1)S(1)}, u32[]{:S(2)}, u32[]{:S(2)}) collective-permute-start(bf16[8,6144]{1,0:T(8,128)(2,1)S(1)} %add_convert_fusion.1), channel_id=1, source_target_pairs={{0,24},{8,16},{16,8},{24,0},{1,25},{9,17},{17,9},{25,1},{2,26},{10... | collective-permute-start | bytes 294920 | tf_op jit(solution)/shard_map/ppermute | solution.py:22
  (31 other events, 214.7 us)
